TPU v7x, 32 devices: a whole 2x2x4 slice. The times are simulated.
32 devices in a mesh: cells: 8 (over z, x), slab: 4 (over y, core).
Axes of the slice: x: 2, y: 2, z: 4, core: 2. Of those that a mesh axis runs over, the one named last changes fastest.
Arguments:
- held_modes: bfloat16 [8192, 1024], P(('cells', 'slab')), may hold values from -5 to 5
- snapshots: bfloat16 [8192, 512], P(('cells', 'slab')), may hold values from -203 to 203
Outputs:
- basis_panel: float32 [8192, 512], P(('cells', 'slab'))
- factor_r: float32 [512, 512], replicated
All inputs are finite; a program needn't handle non-finite values.
Results may differ from a plain program's by a relative error of at most 0.0006.
Values sent between devices are 32-bit elements; how exact they have to be, the bound alone decides.
A program may use at most 64 MiB of HBM per device.

v0:
```python
import jax
import jax.numpy as jnp
from jax import lax
from jax.sharding import PartitionSpec as P


def contract_rows(first, second):
    return lax.dot_general(first, second, (((0,), (0,)), ((), ())), precision=lax.Precision.HIGHEST)


def local(held_modes, snapshots):
    total_rows = held_modes.shape[0] * lax.axis_size("cells") * lax.axis_size("slab")
    local_terms = lax.dot_general(
        held_modes, snapshots, (((0,), (0,)), ((), ())), preferred_element_type=jnp.float32
    )
    summed = lax.psum(local_terms, ("cells", "slab"))
    coefficients = summed / total_rows
    residual_panel = snapshots.astype(jnp.float32) - jnp.dot(
        held_modes.astype(jnp.float32), coefficients, precision=lax.Precision.HIGHEST
    )
    local_gram = contract_rows(residual_panel, residual_panel)
    gram = lax.psum(local_gram, ("cells", "slab")) / total_rows
    lower_factor = jnp.linalg.cholesky(gram)
    basis_panel = lax.linalg.triangular_solve(
        lower_factor, residual_panel, left_side=False, lower=True, transpose_a=True
    )
    return (basis_panel, lower_factor.T)


def solution(mesh):
    in_specs = (P(("cells", "slab"), None), P(("cells", "slab"), None))
    out_specs = (P(("cells", "slab"), None), P())
    return jax.shard_map(local, mesh=mesh, in_specs=in_specs, out_specs=out_specs, check_vma=False)
```

profile of v0, /device:TPU:1, one launch (start us, length us, event | category | flops | bytes accessed | tf_op | source)
XLA Modules:
  0.0 442.4 jit_solution(11196961049046424265)
XLA Ops:
  8.2 2.7 fusion.43
  11.1 137.1 %all-reduce.4.cloned.1.call-done = f32[1024,512]{1,0:T(8,128)} async-done(((f32[1024,512]{1,0:T(8,128)}), f32[1024,512]{1,0:T(8,128)}) %all-reduce.4.cloned.1.call-update) | async-done | bytes 2097168 | tf_op jit(solution)/shard_map/psum | solution.py:16
  148.3 3.4 fusion.5
  151.7 2.0 fusion.44
  153.8 130.0 %all-reduce.6.cloned.1.call-done = f32[512,512]{0,1:T(8,128)} async-done(((f32[512,512]{0,1:T(8,128)}), f32[512,512]{0,1:T(8,128)}) %all-reduce.6.cloned.1.call-update) | async-done | bytes 1048592 | tf_op jit(solution)/shard_map/psum | solution.py:22
  283.8 2.4 broadcast_multiply_fusion
  286.2 1.6 copy.6
  289.0 11.7 %cholesky.104 = f32[128,128]{1,0:T(8,128)S(1)} custom-call(f32[128,128]{1,0:T(8,128)S(1)} %cholesky.266), custom_call_target="Cholesky" | custom-call | tf_op jit(solution)/shard_map/jit(cholesky)/cholesky | solution.py:23
  300.7 9.8 %custom-call.30 = f32[1,128,128]{1,2,0:T(8,128)S(1)} custom-call(f32[1,128,128]{2,1,0:T(8,128)S(1)} %get-tuple-element.33), custom_call_target="InvertDiagBlocksLowerTriangular" | custom-call | tf_op jit(solution)/shard_map/jit(cholesky)/cholesky | solution.py:23
  311.9 1.3 convolution_subtract_fusion
  313.2 11.9 %cholesky.217 = f32[128,128]{1,0:T(8,128)S(1)} custom-call(f32[128,128]{1,0:T(8,128)S(1)} %cholesky.270), custom_call_target="Cholesky" | custom-call | tf_op jit(solution)/shard_map/jit(cholesky)/cholesky | solution.py:23
  325.1 9.8 %custom-call.31 = f32[1,128,128]{1,2,0:T(8,128)S(1)} custom-call(f32[1,128,128]{2,1,0:T(8,128)S(1)} %get-tuple-element.30), custom_call_target="InvertDiagBlocksLowerTriangular" | custom-call | tf_op jit(solution)/shard_map/jit(cholesky)/cholesky | solution.py:23
  335.2 1.3 convolution_subtract_fusion.3
  336.5 11.7 %cholesky.238 = f32[128,128]{1,0:T(8,128)S(1)} custom-call(f32[128,128]{1,0:T(8,128)S(1)} %cholesky.275), custom_call_target="Cholesky" | custom-call | tf_op jit(solution)/shard_map/jit(cholesky)/cholesky | solution.py:23
  348.9 9.8 %custom-call.32 = f32[1,128,128]{1,2,0:T(8,128)S(1)} custom-call(f32[1,128,128]{2,1,0:T(8,128)S(1)} %get-tuple-element.27), custom_call_target="InvertDiagBlocksLowerTriangular" | custom-call | tf_op jit(solution)/shard_map/jit(cholesky)/cholesky | solution.py:23
  360.2 11.9 %cholesky.255 = f32[128,128]{1,0:T(8,128)S(1)} custom-call(f32[128,128]{1,0:T(8,128)S(1)} %convolution_subtract_fusion.5), custom_call_target="Cholesky" | custom-call | tf_op jit(solution)/shard_map/jit(cholesky)/cholesky | solution.py:23
  377.2 11.7 %while.1 = (s32[]{:T(128)}, f32[512,512]{1,0:T(8,128)}, s32[4,2]{0,1:T(2,128)S(1)}, f32[4,128,128]{2,1,0:T(8,128)S(1)}, s32[]{:T(128)}) while((s32[]{:T(128)}, f32[512,512]{1,0:T(8,128)}, s32[4,2]{0,1:T(2,128)S(1)}, f32[4,128,128]{2,1,0:T(8,128)S(1)}, s32[]{:T(128)}) %tuple.33), condition=%wide.while_cond, body=%wide.while_body.sunk | while | flops 2 | bytes 131181 | solution.py:24
  377.9 2.2 bitcast_dynamic-update-slice_fusion.2
  380.9 2.2 bitcast_dynamic-update-slice_fusion.2
  383.8 2.2 bitcast_dynamic-update-slice_fusion.2
  386.7 2.2 bitcast_dynamic-update-slice_fusion.2
  388.9 39.3 %custom-call.33 = f32[4,128,128]{1,2,0:T(8,128)S(1)} custom-call(f32[4,128,128]{2,1,0:T(8,128)S(1)} %get-tuple-element.9), custom_call_target="InvertDiagBlocksLowerTriangular" | custom-call | tf_op jit(solution)/shard_map/triangular_solve | solution.py:24
  431.6 1.3 convolution_subtract_fusion.1
  434.3 1.3 copy.8
  (49 shorter events, 16.2 us)
Async XLA Ops:
  7.2 1.0 copy-start
  7.2 3.8 copy-start.3
  7.2 141.1 %all-reduce.4.cloned.1.call-start = ((), (), s32[]{:S(2)}) async-start(), calls=%async_computation | async-start | bytes 4194304 | tf_op jit(solution)/shard_map/psum | solution.py:16
  10.9 272.8 %all-reduce.6.cloned.1.call-start = ((), (), s32[]{:S(2)}) async-start(), calls=%async_computation.1 | async-start | bytes 2097152 | tf_op jit(solution)/shard_map/psum | solution.py:22
  283.8 3.9 copy-start.1
  288.0 1.0 copy-start.2
Sparse Core Ops, SparseCore 0:
  13.4 134.8 all-reduce.3
  154.9 128.8 all-reduce.5
where the time goes:
time: 445 us; the launch traced here: 442 us
  waiting for transfers between devices  267 us (60%)
  other arithmetic  122 us (27%)
  matrix products  18.5 us (4%)
  local copies, waits for them, and re-layouts  17.7 us (4%)
  between operations  16.8 us (4%)
    psum x1, waiting for transfers between devices, local(): summed = lax.psum(local_terms, ('cells', 'slab'))  137 us
    psum x1, waiting for transfers between devices, local(): gram = lax.psum(local_gram, ('cells', 'slab')) / total_rows  130 us
    another operation x14, other arithmetic, local(): lower_factor = jnp.linalg.cholesky(gram)  78.8 us
    another operation x3, other arithmetic, local(): lax.linalg.triangular_solve(lower_factor, residual_panel, left_side=False...  39.4 us
    another operation x12, local copies, waits for them, and re-layouts  11.6 us
  transfers between devices with their start and end apart: 2, of which 2 were waited for; matrix products, arithmetic and copies ran while one was open for 0% of the time, Pallas kernels for 0%

commit v1 on v0

v1 whole, which is shorter than its diff:
```python
import functools

import jax
import jax.numpy as jnp
from jax import lax
from jax.experimental import pallas as pl
from jax.experimental.pallas import tpu as pltpu
from jax.sharding import PartitionSpec as P

BLOCK = 128
HIGHEST = lax.Precision.HIGHEST


def dot(first, second, dims):
    return lax.dot_general(
        first, second, ((dims[:1], dims[1:]), ((), ())), precision=HIGHEST, preferred_element_type=jnp.float32
    )


def factor_block(rows):
    groups = len(rows)
    lane = lax.broadcasted_iota(jnp.int32, (8, BLOCK), 1)
    sub = lax.broadcasted_iota(jnp.int32, (8, BLOCK), 0)
    rows = list(rows)
    upper, inverse = [], []

    def lanes(value, index):
        return jnp.broadcast_to(value[:, index : index + 1], (8, BLOCK))

    def subs(value, index):
        return jnp.broadcast_to(value[index : index + 1, :], (8, BLOCK))

    for group in range(groups):
        first = 8 * group
        panel = rows[group]
        columns = [lanes(panel, first + k) for k in range(8)]
        outer = [[lanes(rows[other], first + k) for k in range(8)] for other in range(group + 1, groups)]
        scaled = jnp.zeros((8, BLOCK), jnp.float32)
        diagonal = jnp.zeros((8, BLOCK), jnp.float32)
        for j in range(8):
            here = sub == j
            column = columns[j]
            root = lax.rsqrt(subs(column, j))
            scaled_row = subs(panel, j) * root
            scaled = jnp.where(here, scaled_row, scaled)
            diagonal = jnp.where(here, root, diagonal)
            pivot_row = jnp.where(lane == first + j, root, scaled_row) * root
            weight = jnp.where(here, -1.0, column)
            panel = jnp.where(here | (lane == first + j), 0.0, panel) - weight * pivot_row
            for k in range(j + 1, 8):
                entry = subs(columns[k], j) * (root * root)
                columns[k] = jnp.where(here, 0.0, columns[k]) - weight * entry
        row_index = sub + first
        upper.append(jnp.where(lane >= row_index, scaled, 0.0))
        inverse.append(jnp.where(lane < row_index, scaled, jnp.where(lane == row_index, diagonal, 0.0)))
        solved = [subs(panel, k) for k in range(8)]
        kept = (lane < first) | (lane >= first + 8)
        for other in range(group + 1, groups):
            terms = [outer[other - group - 1][k] * solved[k] for k in range(8)]
            while len(terms) > 1:
                terms = [a + b for a, b in zip(terms[::2], terms[1::2])]
            rows[other] = jnp.where(kept, rows[other], 0.0) - terms[0]
    return jnp.concatenate(upper, 0), jnp.concatenate(inverse, 0)


def factor_kernel(gram_ref, panel_ref, basis_ref, factor_ref, schur, residual):
    size = gram_ref.shape[0]
    schur[...] = gram_ref[...]
    residual[...] = panel_ref[...]
    column = lax.broadcasted_iota(jnp.int32, (BLOCK, size), 1)

    def step(block, carry):
        start = pl.multiple_of(block * BLOCK, BLOCK)
        here = pl.ds(start, BLOCK)
        rows = [schur[pl.ds(pl.multiple_of(start + 8 * g, 8), 8), here] for g in range(BLOCK // 8)]
        upper, inverse = factor_block(rows)
        beyond = dot(inverse, schur[here, :], (1, 0))
        beyond = jnp.where(column >= start + BLOCK, beyond, 0.0)
        schur[...] -= dot(beyond, beyond, (0, 0))
        factor_ref[here, :] = beyond
        factor_ref[here, here] = upper
        part = dot(residual[:, here], inverse, (1, 1))
        basis_ref[:, here] = part
        residual[...] -= dot(part, beyond, (1, 0))
        return carry

    lax.fori_loop(0, size // BLOCK, step, 0)


def factor(gram, residual_panel):
    rows, size = residual_panel.shape
    return pl.pallas_call(
        factor_kernel,
        out_shape=(
            jax.ShapeDtypeStruct((rows, size), jnp.float32),
            jax.ShapeDtypeStruct((size, size), jnp.float32),
        ),
        in_specs=[pl.BlockSpec(memory_space=pltpu.VMEM)] * 2,
        out_specs=(pl.BlockSpec(memory_space=pltpu.VMEM),) * 2,
        scratch_shapes=[pltpu.VMEM((size, size), jnp.float32), pltpu.VMEM((rows, size), jnp.float32)],
        compiler_params=pltpu.CompilerParams(vmem_limit_bytes=32 * 1024 * 1024),
        name="factor",
    )(gram, residual_panel)


def local(held_modes, snapshots):
    total_rows = held_modes.shape[0] * lax.axis_size("cells") * lax.axis_size("slab")
    local_terms = lax.dot_general(
        held_modes, snapshots, (((0,), (0,)), ((), ())), preferred_element_type=jnp.float32
    )
    summed = lax.psum(local_terms, ("cells", "slab"))
    coefficients = summed / total_rows
    residual_panel = snapshots.astype(jnp.float32) - jnp.dot(
        held_modes.astype(jnp.float32), coefficients, precision=HIGHEST
    )
    gram = lax.psum(dot(residual_panel, residual_panel, (0, 0)), ("cells", "slab")) / total_rows
    return factor(gram, residual_panel)


def solution(mesh):
    in_specs = (P(("cells", "slab"), None), P(("cells", "slab"), None))
    out_specs = (P(("cells", "slab"), None), P())
    return jax.shard_map(local, mesh=mesh, in_specs=in_specs, out_specs=out_specs, check_vma=False)
```

time: 445 us -> 321 us (0.72)
  other arithmetic: 122 us -> 1.32 us
  Pallas kernels: 0 us -> 27.2 us
  local copies, waits for them, and re-layouts: 17.7 us -> 0.99 us
  matrix products: 18.5 us -> 7.53 us
    another operation x17 -> x0, other arithmetic: 118 us -> none  [the longest x14 78.8 us: local(): lower_factor = jnp.linalg.cholesky(gram)]
    pallas_call x0 -> x1, Pallas kernels: none -> 27.2 us  [factor(): pl.pallas_call(factor_kernel, out_shape=(jax.ShapeDtypeStruct((rows, size...]
    another operation x17 -> x0, local copies, waits for them, and re-layouts: 11.8 us -> none
    another operation x13 -> x0, matrix products: 10.4 us -> none  [the longest x6 5.46 us: local(): lower_factor = jnp.linalg.cholesky(gram)]
where the time goes in v1:
time: 321 us; the launch traced here: 319 us
  waiting for transfers between devices  268 us (83%)
  Pallas kernels  27.2 us (8%)
  between operations  14.1 us (4%)
  matrix products  7.53 us (2%)
    psum x1, waiting for transfers between devices, local(): summed = lax.psum(local_terms, ('cells', 'slab'))  137 us
    psum x1, waiting for transfers between devices, local(): lax.psum(dot(residual_panel, residual_panel, (0, 0)), ('cells', 'slab'))  131 us
    pallas_call x1, Pallas kernels, factor(): pl.pallas_call(factor_kernel, out_shape=(jax.ShapeDtypeStruct((rows, size...  27.2 us
  transfers between devices with their start and end apart: 2, of which 2 were waited for; matrix products, arithmetic and copies ran while one was open for 0% of the time, Pallas kernels for 0%

profile of v1, /device:TPU:1, one launch (start us, length us, event | category | flops | bytes accessed | tf_op | source)
XLA Modules:
  0.0 319.1 jit_solution(14221122762412990392)
XLA Ops:
  7.2 0.0 copy-start
  7.2 0.0 copy-start.1
  7.2 0.0 all-reduce.3.cloned.1.call-start
  7.2 1.0 copy-done
  8.2 2.7 fusion.10
  10.9 0.0 all-reduce.3.cloned.1.call-update
  11.0 0.0 all-reduce.5.cloned.1.call-start
  11.0 137.2 %all-reduce.3.cloned.1.call-done = f32[1024,512]{1,0:T(8,128)} async-done(((f32[1024,512]{1,0:T(8,128)}), f32[1024,512]{1,0:T(8,128)}) %all-reduce.3.cloned.1.call-update) | async-done | bytes 2097168 | tf_op jit(solution)/shard_map/psum | solution.py:111
  148.2 0.0 copy-done.1
  148.2 2.8 fusion.5.panel_ref
  151.0 2.0 fusion.11
  153.0 0.0 all-reduce.5.cloned.1.call-update
  153.1 130.7 %all-reduce.5.cloned.1.call-done = f32[512,512]{1,0:T(8,128)} async-done(((f32[512,512]{1,0:T(8,128)}), f32[512,512]{1,0:T(8,128)}) %all-reduce.5.cloned.1.call-update) | async-done | bytes 1048592 | tf_op jit(solution)/shard_map/psum | solution.py:116
  283.7 1.3 broadcast_multiply_fusion.gram_ref
  285.0 27.2 %factor.1 = (f32[256,512]{1,0:T(8,128)}, f32[512,512]{1,0:T(8,128)}) custom-call(f32[512,512]{1,0:T(8,128)S(1)} %broadcast_multiply_fusion.gram_ref, f32[256,512]{1,0:T(8,128)S(1)} %fusion.5.panel_ref), custom_call_target="tpu_custom_call" | custom-call | tf_op jit(solution)/shard_map/factor/pallas_call | solution.py:92
Async XLA Ops:
  7.2 1.0 copy-start
  7.2 141.1 %copy-start.1 = (bf16[256,512]{1,0:T(8,128)(2,1)S(1)}, bf16[256,512]{1,0:T(8,128)(2,1)}, u32[]{:S(2)}) copy-start(bf16[256,512]{1,0:T(8,128)(2,1)} %param.3) | copy-start | bytes 786436
  7.2 141.0 %all-reduce.3.cloned.1.call-start = ((), (), s32[]{:S(2)}) async-start(), calls=%async_computation | async-start | bytes 4194304 | tf_op jit(solution)/shard_map/psum | solution.py:111
  11.0 272.8 %all-reduce.5.cloned.1.call-start = ((), (), s32[]{:S(2)}) async-start(), calls=%async_computation.1 | async-start | bytes 2097152 | tf_op jit(solution)/shard_map/psum | solution.py:116
Sparse Core Ops, SparseCore 0:
  13.4 134.8 all-reduce.2
  154.8 128.8 all-reduce.4

commit v2 on v1

--- a/solution.py
+++ b/solution.py
@@ -8,6 +8,7 @@
 from jax.sharding import PartitionSpec as P
 
 BLOCK = 128
+MESH = pl.DeviceIdType.MESH
 HIGHEST = lax.Precision.HIGHEST
 
 
@@ -63,9 +64,229 @@
     return jnp.concatenate(upper, 0), jnp.concatenate(inverse, 0)
 
 
+def upper_blocks(size):
+    count = size // BLOCK
+    return [(i, j) for i in range(count) for j in range(i, count)]
+
+
+class Part:
+    def __init__(self, start, rows, stages, sems):
+        self.start, self.rows, self.stages, self.sems = start, rows, stages, sems
+        self.spans = [(start, rows)]
+        for stage in stages:
+            at, n = self.spans[-1]
+            n //= stage["count"]
+            self.spans.append((at + stage["index"] * n, n))
+
+
+def slice_of(start, rows):
+    return pl.ds(pl.multiple_of(start, 8), rows)
+
+
+def all_reduce(acc, total, landing, places, produce, scale, send_sems, recv_sems, started):
+    core, pair, plane, line = places
+    half = acc.shape[0] // 2
+    unit = 8 * plane["count"] * line["count"]
+    long_rows = max(1, round(0.75 * (half // unit))) * unit
+    used = [0]
+
+    def copy(src, dst, device):
+        index = used[0]
+        used[0] += 1
+        descriptor = pltpu.make_async_remote_copy(
+            src_ref=src,
+            dst_ref=dst,
+            send_sem=send_sems.at[index],
+            recv_sem=recv_sems.at[index],
+            device_id=device,
+            device_id_type=MESH,
+        )
+        descriptor.start()
+        started.append(descriptor)
+        return descriptor
+
+    mine, other = core * half, (1 - core) * half
+    bounds = [(0, long_rows, (plane, line))]
+    if half > long_rows:
+        bounds.append((long_rows, half - long_rows, (line, plane)))
+    parts = [Part(mine + at, n, stages, None) for at, n, stages in bounds]
+    slot = [0]
+
+    def room(count, rows):
+        at = slot[0]
+        slot[0] += count * rows
+        return [landing.at[pl.ds(at + k * rows, rows)] for k in range(count)]
+
+    firsts = []
+    for at, n, _ in bounds:
+        produce(other + at, n)
+        span = room(1, n)[0]
+        firsts.append((copy(acc.at[slice_of(other + at, n)], span, pair), span))
+    for at, n, _ in bounds:
+        produce(mine + at, n)
+    for part, (first, span) in zip(parts, firsts):
+        first.wait_recv()
+        where = slice_of(part.start, part.rows)
+        acc[where, :] = acc[where, :] + span[...]
+
+    def send_scatter(part, level):
+        stage = part.stages[level]
+        at, _ = part.spans[level]
+        n = part.spans[level + 1][1]
+        spans = room(stage["count"] - 1, n)
+        part.pending = [
+            (copy(acc.at[slice_of(at + target * n, n)], span, device), span)
+            for (target, device, _), span in zip(stage["peers"], spans)
+        ]
+
+    def finish_scatter(part, level):
+        where = slice_of(*part.spans[level + 1])
+        value = acc[where, :]
+        for descriptor, span in part.pending:
+            descriptor.wait_recv()
+            value = value + span[...]
+        if level + 1 == len(part.stages):
+            total[where, :] = value * scale
+        else:
+            acc[where, :] = value
+
+    def send_gather(part, level):
+        where = slice_of(*part.spans[level + 1])
+        part.pending = [
+            copy(total.at[where], total.at[where], device) for _, device, _ in part.stages[level]["peers"]
+        ]
+
+    lasts = []
+
+    def forward(start, n):
+        where = slice_of(start, n)
+        lasts.append(copy(total.at[where], total.at[where], pair))
+
+    for part in parts:
+        send_scatter(part, 0)
+    for part in parts[::-1]:
+        finish_scatter(part, 0)
+        send_scatter(part, 1)
+    for part in parts[::-1]:
+        finish_scatter(part, 1)
+        send_gather(part, 1)
+    for part in parts[::-1]:
+        for descriptor in part.pending:
+            descriptor.wait_recv()
+        send_gather(part, 0)
+        forward(*part.spans[1])
+    for part in parts[::-1]:
+        at, _ = part.spans[0]
+        n = part.spans[1][1]
+        for descriptor, (_, _, source) in zip(part.pending, part.stages[0]["peers"]):
+            descriptor.wait_recv()
+            forward(at + source * n, n)
+    for descriptor in lasts:
+        descriptor.wait_recv()
+
+
+def panel_kernel(
+    line_count, total_rows, modes_ref, snaps_ref, residual_ref, gram_ref,
+    terms, coefficients, landing, gram_terms, gram, gram_landing, send_sems, recv_sems, gram_send_sems, gram_recv_sems,
+):
+    cells, slab = lax.axis_index("cells"), lax.axis_index("slab")
+    z, x, y, core = cells // 2, cells % 2, slab // 2, slab % 2
+    pair = {"cells": cells, "slab": y * 2 + (1 - core)}
+    plane_peers = []
+    for k in range(1, 4):
+        there_x = 1 - x if k & 2 else x
+        there_y = 1 - y if k & 1 else y
+        device = {"cells": z * 2 + there_x, "slab": there_y * 2 + core}
+        plane_peers.append((there_x * 2 + there_y, device, there_x * 2 + there_y))
+    line_peers = []
+    for k in range(1, line_count):
+        ahead, behind = lax.rem(z + k, line_count), lax.rem(z + line_count - k, line_count)
+        line_peers.append((ahead, {"cells": ahead * 2 + x, "slab": slab}, behind))
+    plane = {"count": 4, "index": x * 2 + y, "peers": plane_peers}
+    line = {"count": line_count, "index": z, "peers": line_peers}
+    places = (core, pair, plane, line)
+
+    devices = [pair] + [peer[1] for peer in plane_peers + line_peers]
+    barrier = pltpu.get_barrier_semaphore()
+    for device in devices:
+        pl.semaphore_signal(barrier, inc=1, device_id=device, device_id_type=MESH)
+
+    started = []
+    scale = 1.0 / total_rows
+    entered = []
+
+    def project(start, rows):
+        wanted = modes_ref[:, pl.ds(pl.multiple_of(start, BLOCK), rows)]
+        terms[slice_of(start, rows), :] = lax.dot_general(
+            wanted, snaps_ref[...], (((0,), (0,)), ((), ())), preferred_element_type=jnp.float32
+        )
+        if not entered:
+            pl.semaphore_wait(barrier, len(devices))
+            entered.append(True)
+
+    all_reduce(terms, coefficients, landing, places, project, scale, send_sems, recv_sems, started)
+
+    def times(part):
+        return jnp.dot(modes_ref[...], part, preferred_element_type=jnp.float32)
+
+    whole = coefficients[...]
+    high = whole.astype(jnp.bfloat16)
+    rest = whole - high.astype(jnp.float32)
+    middle = rest.astype(jnp.bfloat16)
+    low = (rest - middle.astype(jnp.float32)).astype(jnp.bfloat16)
+    residual_ref[...] = snaps_ref[...].astype(jnp.float32) - (times(high) + (times(middle) + times(low)))
+
+    size = residual_ref.shape[1]
+    blocks = upper_blocks(size)
+    for i in range(size // BLOCK):
+        row = dot(residual_ref[:, i * BLOCK : (i + 1) * BLOCK], residual_ref[:, i * BLOCK :], (0, 0))
+        for j in range(i, size // BLOCK):
+            at = blocks.index((i, j)) * BLOCK
+            gram_terms[at : at + BLOCK, :] = row[:, (j - i) * BLOCK : (j - i + 1) * BLOCK]
+    all_reduce(
+        gram_terms, gram, gram_landing, places, lambda start, rows: None, scale, gram_send_sems, gram_recv_sems, started
+    )
+    gram_ref[...] = gram[...]
+    for descriptor in started:
+        descriptor.wait_send()
+
+
+def panel(held_modes, snapshots, line_count, total_rows):
+    rows, modes = held_modes.shape
+    size = snapshots.shape[1]
+    gram_rows = len(upper_blocks(size)) * BLOCK
+    count = 2 * (1 + 2 * (3 + line_count - 1) + max(4, line_count))
+    sems = pltpu.SemaphoreType.DMA((count,))
+    return pl.pallas_call(
+        functools.partial(panel_kernel, line_count, total_rows),
+        out_shape=(
+            jax.ShapeDtypeStruct((rows, size), jnp.float32),
+            jax.ShapeDtypeStruct((gram_rows, BLOCK), jnp.float32),
+        ),
+        in_specs=[pl.BlockSpec(memory_space=pltpu.VMEM)] * 2,
+        out_specs=(pl.BlockSpec(memory_space=pltpu.VMEM),) * 2,
+        scratch_shapes=[
+            pltpu.VMEM((modes, size), jnp.float32),
+            pltpu.VMEM((modes, size), jnp.float32),
+            pltpu.VMEM((2 * modes, size), jnp.float32),
+            pltpu.VMEM((gram_rows, BLOCK), jnp.float32),
+            pltpu.VMEM((gram_rows, BLOCK), jnp.float32),
+            pltpu.VMEM((2 * gram_rows, BLOCK), jnp.float32),
+            sems, sems, sems, sems,
+        ],
+        compiler_params=pltpu.CompilerParams(
+            collective_id=0, has_side_effects=True, vmem_limit_bytes=40 * 1024 * 1024
+        ),
+        name="panel",
+    )(held_modes, snapshots)
+
+
 def factor_kernel(gram_ref, panel_ref, basis_ref, factor_ref, schur, residual):
-    size = gram_ref.shape[0]
-    schur[...] = gram_ref[...]
+    size = schur.shape[0]
+    schur[...] = jnp.zeros_like(schur)
+    for index, (i, j) in enumerate(upper_blocks(size)):
+        block = gram_ref[index * BLOCK : (index + 1) * BLOCK, :]
+        schur[i * BLOCK : (i + 1) * BLOCK, j * BLOCK : (j + 1) * BLOCK] = block
     residual[...] = panel_ref[...]
     column = lax.broadcasted_iota(jnp.int32, (BLOCK, size), 1)
 
@@ -104,17 +325,25 @@
 
 
 def local(held_modes, snapshots):
-    total_rows = held_modes.shape[0] * lax.axis_size("cells") * lax.axis_size("slab")
+    cells, slab = lax.axis_size("cells"), lax.axis_size("slab")
+    total_rows = held_modes.shape[0] * cells * slab
+    size = snapshots.shape[1]
+    blocks = upper_blocks(size)
+    line_count = cells // 2
+    unit = 8 * 4 * line_count
+    halves = (held_modes.shape[1] // 2, len(blocks) * BLOCK // 2)
+    if slab == 4 and cells % 2 == 0 and all(half % unit == 0 for half in halves):
+        return factor(*panel(held_modes, snapshots, line_count, total_rows)[::-1])
     local_terms = lax.dot_general(
         held_modes, snapshots, (((0,), (0,)), ((), ())), preferred_element_type=jnp.float32
     )
-    summed = lax.psum(local_terms, ("cells", "slab"))
-    coefficients = summed / total_rows
+    coefficients = lax.psum(local_terms, ("cells", "slab")) / total_rows
     residual_panel = snapshots.astype(jnp.float32) - jnp.dot(
         held_modes.astype(jnp.float32), coefficients, precision=HIGHEST
     )
     gram = lax.psum(dot(residual_panel, residual_panel, (0, 0)), ("cells", "slab")) / total_rows
-    return factor(gram, residual_panel)
+    packed = [gram[i * BLOCK : (i + 1) * BLOCK, j * BLOCK : (j + 1) * BLOCK] for i, j in blocks]
+    return factor(jnp.concatenate(packed, 0), residual_panel)
 
 
 def solution(mesh):

time: 321 us -> 94.8 us (0.30)
  waiting for transfers between devices: 268 us -> 0 us
  Pallas kernels: 27.2 us -> 91.9 us
  between operations: 14.1 us -> 0.65 us
  matrix products: 7.53 us -> 0 us
    psum x2 -> x0, waiting for transfers between devices: 268 us -> none  [the longest x1 137 us: local(): summed = lax.psum(local_terms, ('cells', 'slab'))]
    pallas_call x0 -> x1, Pallas kernels: none -> 64.7 us  [panel(): pl.pallas_call(functools.partial(panel_kernel, line_count, total_rows), o...]
    dot_general x3 -> x0, matrix products: 7.53 us -> none  [the longest x1 2.78 us: local(): jnp.dot(held_modes.astype(jnp.float32), coefficients, precision=HIGHEST)]
  transfers between devices with their start and end apart: 2 -> 0, of which waited for: 2 -> 0; matrix products, arithmetic and copies ran while one was open for 0% -> 0% of each run, Pallas kernels for 0% -> 0%
where the time goes in v2:
time: 94.8 us; the launch traced here: 94.6 us
  Pallas kernels  91.9 us (97%)
  local copies, waits for them, and re-layouts  1.98 us (2%)
    pallas_call x1, Pallas kernels, panel(): pl.pallas_call(functools.partial(panel_kernel, line_count, total_rows), o...  64.7 us
    pallas_call x1, Pallas kernels, factor(): pl.pallas_call(factor_kernel, out_shape=(jax.ShapeDtypeStruct((rows, size...  27.3 us
    unnamed x4, local copies, waits for them, and re-layouts  1.98 us

profile of v2, /device:TPU:1, one launch (start us, length us, event | category | flops | bytes accessed | tf_op | source)
XLA Modules:
  0.0 94.6 jit_solution(12741756941692758959)
XLA Ops:
  0.6 0.0 copy-start
  0.6 1.0 %copy-done = bf16[256,1024]{1,0:T(8,128)(2,1)S(1)} copy-done((bf16[256,1024]{1,0:T(8,128)(2,1)S(1)}, bf16[256,1024]{1,0:T(8,128)(2,1)}, u32[]{:S(2)}) %copy-start) | copy-done | bytes 524312
  1.7 0.0 copy-start.1
  1.7 0.9 %copy-done.1 = bf16[256,512]{1,0:T(8,128)(2,1)S(1)} copy-done((bf16[256,512]{1,0:T(8,128)(2,1)S(1)}, bf16[256,512]{1,0:T(8,128)(2,1)}, u32[]{:S(2)}) %copy-start.1) | copy-done | bytes 262168
  2.6 64.7 %panel.1 = (f32[256,512]{1,0:T(8,128)S(1)}, f32[1280,128]{1,0:T(8,128)S(1)}) custom-call(bf16[256,1024]{1,0:T(8,128)(2,1)S(1)} %copy-done, bf16[256,512]{1,0:T(8,128)(2,1)S(1)} %copy-done.1), custom_call_target="tpu_custom_call" | custom-call | tf_op jit(solution)/shard_map/panel/pallas_call | solution.py:260
  67.3 27.3 %factor.1 = (f32[256,512]{1,0:T(8,128)}, f32[512,512]{1,0:T(8,128)}) custom-call(f32[1280,128]{1,0:T(8,128)S(1)} %get-tuple-element.4.gram_ref, f32[256,512]{1,0:T(8,128)S(1)} %get-tuple-element.5.panel_ref), custom_call_target="tpu_custom_call" | custom-call | tf_op jit(solution)/shard_map/factor/pallas_call | solution.py:313
Async XLA Ops:
  0.6 1.0 %copy-start = (bf16[256,1024]{1,0:T(8,128)(2,1)S(1)}, bf16[256,1024]{1,0:T(8,128)(2,1)}, u32[]{:S(2)}) copy-start(bf16[256,1024]{1,0:T(8,128)(2,1)} %modes_ref.1) | copy-start | bytes 1572868
  1.7 0.9 %copy-start.1 = (bf16[256,512]{1,0:T(8,128)(2,1)S(1)}, bf16[256,512]{1,0:T(8,128)(2,1)}, u32[]{:S(2)}) copy-start(bf16[256,512]{1,0:T(8,128)(2,1)} %snaps_ref.1) | copy-start | bytes 786436

commit v3 on v2

--- a/solution.py
+++ b/solution.py
@@ -9,6 +9,8 @@
 
 BLOCK = 128
 MESH = pl.DeviceIdType.MESH
+CHUNKS = 2
+STEPS = 7
 HIGHEST = lax.Precision.HIGHEST
 
 
@@ -64,14 +66,9 @@
     return jnp.concatenate(upper, 0), jnp.concatenate(inverse, 0)
 
 
-def upper_blocks(size):
-    count = size // BLOCK
-    return [(i, j) for i in range(count) for j in range(i, count)]
-
-
 class Part:
-    def __init__(self, start, rows, stages, sems):
-        self.start, self.rows, self.stages, self.sems = start, rows, stages, sems
+    def __init__(self, start, rows, stages):
+        self.start, self.rows, self.stages, self.pending = start, rows, stages, []
         self.spans = [(start, rows)]
         for stage in stages:
             at, n = self.spans[-1]
@@ -109,25 +106,13 @@
     bounds = [(0, long_rows, (plane, line))]
     if half > long_rows:
         bounds.append((long_rows, half - long_rows, (line, plane)))
-    parts = [Part(mine + at, n, stages, None) for at, n, stages in bounds]
+    parts = [Part(mine + at, n, stages) for at, n, stages in bounds]
     slot = [0]
 
     def room(count, rows):
         at = slot[0]
         slot[0] += count * rows
         return [landing.at[pl.ds(at + k * rows, rows)] for k in range(count)]
-
-    firsts = []
-    for at, n, _ in bounds:
-        produce(other + at, n)
-        span = room(1, n)[0]
-        firsts.append((copy(acc.at[slice_of(other + at, n)], span, pair), span))
-    for at, n, _ in bounds:
-        produce(mine + at, n)
-    for part, (first, span) in zip(parts, firsts):
-        first.wait_recv()
-        where = slice_of(part.start, part.rows)
-        acc[where, :] = acc[where, :] + span[...]
 
     def send_scatter(part, level):
         stage = part.stages[level]
@@ -162,33 +147,55 @@
         where = slice_of(start, n)
         lasts.append(copy(total.at[where], total.at[where], pair))
 
-    for part in parts:
+    firsts = []
+    for at, n, _ in bounds:
+        produce(other + at, n)
+        span = room(1, n)[0]
+        firsts.append((copy(acc.at[slice_of(other + at, n)], span, pair), span))
+    for at, n, _ in bounds:
+        produce(mine + at, n)
+    yield
+    for part, (first, span) in zip(parts, firsts):
+        first.wait_recv()
+        where = slice_of(part.start, part.rows)
+        acc[where, :] = acc[where, :] + span[...]
         send_scatter(part, 0)
-    for part in parts[::-1]:
-        finish_scatter(part, 0)
-        send_scatter(part, 1)
-    for part in parts[::-1]:
-        finish_scatter(part, 1)
-        send_gather(part, 1)
+    yield
+    for level in (0, 1):
+        for part in parts[::-1]:
+            finish_scatter(part, level)
+            if level == 0:
+                send_scatter(part, 1)
+            else:
+                send_gather(part, 1)
+        yield
     for part in parts[::-1]:
         for descriptor in part.pending:
             descriptor.wait_recv()
         send_gather(part, 0)
         forward(*part.spans[1])
+    yield
     for part in parts[::-1]:
         at, _ = part.spans[0]
         n = part.spans[1][1]
         for descriptor, (_, _, source) in zip(part.pending, part.stages[0]["peers"]):
             descriptor.wait_recv()
             forward(at + source * n, n)
+    yield
     for descriptor in lasts:
         descriptor.wait_recv()
 
 
 def panel_kernel(
-    line_count, total_rows, modes_ref, snaps_ref, residual_ref, gram_ref,
-    terms, coefficients, landing, gram_terms, gram, gram_landing, send_sems, recv_sems, gram_send_sems, gram_recv_sems,
+    line_count, total_rows, modes_hbm, snaps_hbm, residual_ref, gram_ref, modes_ref, snaps_ref, load_sems,
+    terms, coefficients, landing, gram_terms, gram, gram_landing, send_sems, recv_sems,
 ):
+    loads = [
+        pltpu.make_async_copy(modes_hbm, modes_ref, load_sems.at[0]),
+        pltpu.make_async_copy(snaps_hbm, snaps_ref, load_sems.at[1]),
+    ]
+    for load in loads:
+        load.start()
     cells, slab = lax.axis_index("cells"), lax.axis_index("slab")
     z, x, y, core = cells // 2, cells % 2, slab // 2, slab % 2
     pair = {"cells": cells, "slab": y * 2 + (1 - core)}
@@ -211,42 +218,72 @@
     for device in devices:
         pl.semaphore_signal(barrier, inc=1, device_id=device, device_id_type=MESH)
 
+    for load in loads:
+        load.wait()
+
     started = []
     scale = 1.0 / total_rows
     entered = []
-
-    def project(start, rows):
-        wanted = modes_ref[:, pl.ds(pl.multiple_of(start, BLOCK), rows)]
-        terms[slice_of(start, rows), :] = lax.dot_general(
-            wanted, snaps_ref[...], (((0,), (0,)), ((), ())), preferred_element_type=jnp.float32
+    size = residual_ref.shape[1]
+    width = size // CHUNKS
+
+    def coefficient_sum(chunk):
+        acc = terms.at[chunk]
+
+        def project(start, rows):
+            wanted = modes_ref[:, pl.ds(pl.multiple_of(start, BLOCK), rows)]
+            acc[slice_of(start, rows), :] = lax.dot_general(
+                wanted, snaps_ref[:, chunk * width : (chunk + 1) * width], (((0,), (0,)), ((), ())),
+                preferred_element_type=jnp.float32,
+            )
+            if not entered:
+                pl.semaphore_wait(barrier, len(devices))
+                entered.append(True)
+
+        return all_reduce(
+            acc, coefficients.at[chunk], landing.at[chunk], places, project, scale,
+            send_sems.at[chunk], recv_sems.at[chunk], started,
         )
-        if not entered:
-            pl.semaphore_wait(barrier, len(devices))
-            entered.append(True)
-
-    all_reduce(terms, coefficients, landing, places, project, scale, send_sems, recv_sems, started)
+
+    def gram_sum(chunk):
+        rows = pl.ds(0, (chunk + 1) * width)
+        return all_reduce(
+            gram_terms.at[chunk, rows], gram.at[chunk, rows], gram_landing.at[chunk], places, lambda start, n: None,
+            scale, send_sems.at[CHUNKS + chunk], recv_sems.at[CHUNKS + chunk], started,
+        )
 
     def times(part):
         return jnp.dot(modes_ref[...], part, preferred_element_type=jnp.float32)
 
-    whole = coefficients[...]
-    high = whole.astype(jnp.bfloat16)
-    rest = whole - high.astype(jnp.float32)
-    middle = rest.astype(jnp.bfloat16)
-    low = (rest - middle.astype(jnp.float32)).astype(jnp.bfloat16)
-    residual_ref[...] = snaps_ref[...].astype(jnp.float32) - (times(high) + (times(middle) + times(low)))
-
-    size = residual_ref.shape[1]
-    blocks = upper_blocks(size)
-    for i in range(size // BLOCK):
-        row = dot(residual_ref[:, i * BLOCK : (i + 1) * BLOCK], residual_ref[:, i * BLOCK :], (0, 0))
-        for j in range(i, size // BLOCK):
-            at = blocks.index((i, j)) * BLOCK
-            gram_terms[at : at + BLOCK, :] = row[:, (j - i) * BLOCK : (j - i + 1) * BLOCK]
-    all_reduce(
-        gram_terms, gram, gram_landing, places, lambda start, rows: None, scale, gram_send_sems, gram_recv_sems, started
-    )
-    gram_ref[...] = gram[...]
+    def subtract(chunk):
+        columns = slice(chunk * width, (chunk + 1) * width)
+        whole = coefficients[chunk]
+        high = whole.astype(jnp.bfloat16)
+        rest = whole - high.astype(jnp.float32)
+        middle = rest.astype(jnp.bfloat16)
+        low = (rest - middle.astype(jnp.float32)).astype(jnp.bfloat16)
+        value = snaps_ref[:, columns].astype(jnp.float32) - (times(high) + (times(middle) + times(low)))
+        residual_ref[:, columns] = value
+        before = (chunk + 1) * width
+        gram_terms[chunk, :before, :] = dot(residual_ref[:, :before], value, (0, 0))
+
+    sums = [coefficient_sum(chunk) for chunk in range(CHUNKS)]
+    gram_sums = [gram_sum(chunk) for chunk in range(CHUNKS)]
+    for _ in range(STEPS - 1):
+        for turn in sums:
+            next(turn)
+    for chunk in range(CHUNKS):
+        next(sums[chunk], None)
+        subtract(chunk)
+        next(gram_sums[chunk])
+    for _ in range(STEPS - 1):
+        for turn in gram_sums:
+            next(turn, None)
+    for chunk in range(CHUNKS):
+        before, columns = (chunk + 1) * width, slice(chunk * width, (chunk + 1) * width)
+        gram_ref[:before, columns] = gram[chunk, :before, :]
+        if before < size:
+            gram_ref[before:, columns] = jnp.zeros((size - before, width), jnp.float32)
     for descriptor in started:
         descriptor.wait_send()
 
@@ -254,25 +291,28 @@
 def panel(held_modes, snapshots, line_count, total_rows):
     rows, modes = held_modes.shape
     size = snapshots.shape[1]
-    gram_rows = len(upper_blocks(size)) * BLOCK
+    width = size // CHUNKS
     count = 2 * (1 + 2 * (3 + line_count - 1) + max(4, line_count))
-    sems = pltpu.SemaphoreType.DMA((count,))
     return pl.pallas_call(
         functools.partial(panel_kernel, line_count, total_rows),
         out_shape=(
             jax.ShapeDtypeStruct((rows, size), jnp.float32),
-            jax.ShapeDtypeStruct((gram_rows, BLOCK), jnp.float32),
+            jax.ShapeDtypeStruct((size, size), jnp.float32),
         ),
-        in_specs=[pl.BlockSpec(memory_space=pltpu.VMEM)] * 2,
+        in_specs=[pl.BlockSpec(memory_space=pl.ANY)] * 2,
         out_specs=(pl.BlockSpec(memory_space=pltpu.VMEM),) * 2,
         scratch_shapes=[
-            pltpu.VMEM((modes, size), jnp.float32),
-            pltpu.VMEM((modes, size), jnp.float32),
-            pltpu.VMEM((2 * modes, size), jnp.float32),
-            pltpu.VMEM((gram_rows, BLOCK), jnp.float32),
-            pltpu.VMEM((gram_rows, BLOCK), jnp.float32),
-            pltpu.VMEM((2 * gram_rows, BLOCK), jnp.float32),
-            sems, sems, sems, sems,
+            pltpu.VMEM((rows, modes), held_modes.dtype),
+            pltpu.VMEM((rows, size), snapshots.dtype),
+            pltpu.SemaphoreType.DMA((2,)),
+            pltpu.VMEM((CHUNKS, modes, width), jnp.float32),
+            pltpu.VMEM((CHUNKS, modes, width), jnp.float32),
+            pltpu.VMEM((CHUNKS, 2 * modes, width), jnp.float32),
+            pltpu.VMEM((CHUNKS, size, width), jnp.float32),
+            pltpu.VMEM((CHUNKS, size, width), jnp.float32),
+            pltpu.VMEM((CHUNKS, 2 * size, width), jnp.float32),
+            pltpu.SemaphoreType.DMA((2 * CHUNKS, count)),
+            pltpu.SemaphoreType.DMA((2 * CHUNKS, count)),
         ],
         compiler_params=pltpu.CompilerParams(
             collective_id=0, has_side_effects=True, vmem_limit_bytes=40 * 1024 * 1024
@@ -282,11 +322,8 @@
 
 
 def factor_kernel(gram_ref, panel_ref, basis_ref, factor_ref, schur, residual):
-    size = schur.shape[0]
-    schur[...] = jnp.zeros_like(schur)
-    for index, (i, j) in enumerate(upper_blocks(size)):
-        block = gram_ref[index * BLOCK : (index + 1) * BLOCK, :]
-        schur[i * BLOCK : (i + 1) * BLOCK, j * BLOCK : (j + 1) * BLOCK] = block
+    size = gram_ref.shape[0]
+    schur[...] = gram_ref[...]
     residual[...] = panel_ref[...]
     column = lax.broadcasted_iota(jnp.int32, (BLOCK, size), 1)
 
@@ -328,11 +365,10 @@
     cells, slab = lax.axis_size("cells"), lax.axis_size("slab")
     total_rows = held_modes.shape[0] * cells * slab
     size = snapshots.shape[1]
-    blocks = upper_blocks(size)
     line_count = cells // 2
     unit = 8 * 4 * line_count
-    halves = (held_modes.shape[1] // 2, len(blocks) * BLOCK // 2)
-    if slab == 4 and cells % 2 == 0 and all(half % unit == 0 for half in halves):
+    halves = (held_modes.shape[1] // 2, size // CHUNKS // 2)
+    if slab == 4 and cells % 2 == 0 and size % (CHUNKS * BLOCK) == 0 and all(half % unit == 0 for half in halves):
         return factor(*panel(held_modes, snapshots, line_count, total_rows)[::-1])
     local_terms = lax.dot_general(
         held_modes, snapshots, (((0,), (0,)), ((), ())), preferred_element_type=jnp.float32
@@ -342,8 +378,7 @@
         held_modes.astype(jnp.float32), coefficients, precision=HIGHEST
     )
     gram = lax.psum(dot(residual_panel, residual_panel, (0, 0)), ("cells", "slab")) / total_rows
-    packed = [gram[i * BLOCK : (i + 1) * BLOCK, j * BLOCK : (j + 1) * BLOCK] for i, j in blocks]
-    return factor(jnp.concatenate(packed, 0), residual_panel)
+    return factor(gram, residual_panel)
 
 
 def solution(mesh):

time: 94.8 us -> 89.9 us (0.948)
  Pallas kernels: 91.9 us -> 87.1 us
    pallas_call x1, Pallas kernels: 64.7 us -> 59.8 us  [panel(): pl.pallas_call(functools.partial(panel_kernel, line_count, total_rows), o...]
where the time goes in v3:
time: 89.9 us; the launch traced here: 89.7 us
  Pallas kernels  87.1 us (97%)
  local copies, waits for them, and re-layouts  1.98 us (2%)
    pallas_call x1, Pallas kernels, panel(): pl.pallas_call(functools.partial(panel_kernel, line_count, total_rows), o...  59.8 us
    pallas_call x1, Pallas kernels, factor(): pl.pallas_call(factor_kernel, out_shape=(jax.ShapeDtypeStruct((rows, size...  27.3 us
    unnamed x4, local copies, waits for them, and re-layouts  1.98 us

profile of v3, /device:TPU:1, one launch (start us, length us, event | category | flops | bytes accessed | tf_op | source)
XLA Modules:
  0.0 89.7 jit_solution(16124292103577803500)
XLA Ops:
  0.6 0.0 copy-start
  0.6 1.0 %copy-done = bf16[256,1024]{1,0:T(8,128)(2,1)S(1)} copy-done((bf16[256,1024]{1,0:T(8,128)(2,1)S(1)}, bf16[256,1024]{1,0:T(8,128)(2,1)}, u32[]{:S(2)}) %copy-start) | copy-done | bytes 524312
  1.7 0.0 copy-start.1
  1.7 0.9 %copy-done.1 = bf16[256,512]{1,0:T(8,128)(2,1)S(1)} copy-done((bf16[256,512]{1,0:T(8,128)(2,1)S(1)}, bf16[256,512]{1,0:T(8,128)(2,1)}, u32[]{:S(2)}) %copy-start.1) | copy-done | bytes 262168
  2.6 59.8 %panel.1 = (f32[256,512]{1,0:T(8,128)S(1)}, f32[512,512]{1,0:T(8,128)S(1)}) custom-call(bf16[256,1024]{1,0:T(8,128)(2,1)S(1)} %copy-done, bf16[256,512]{1,0:T(8,128)(2,1)S(1)} %copy-done.1), custom_call_target="tpu_custom_call" | custom-call | tf_op jit(solution)/shard_map/panel/pallas_call | solution.py:296
  62.5 27.3 %factor.1 = (f32[256,512]{1,0:T(8,128)}, f32[512,512]{1,0:T(8,128)}) custom-call(f32[512,512]{1,0:T(8,128)S(1)} %get-tuple-element.4.gram_ref, f32[256,512]{1,0:T(8,128)S(1)} %get-tuple-element.5.panel_ref), custom_call_target="tpu_custom_call" | custom-call | tf_op jit(solution)/shard_map/factor/pallas_call | solution.py:350
Async XLA Ops:
  0.6 1.0 %copy-start = (bf16[256,1024]{1,0:T(8,128)(2,1)S(1)}, bf16[256,1024]{1,0:T(8,128)(2,1)}, u32[]{:S(2)}) copy-start(bf16[256,1024]{1,0:T(8,128)(2,1)} %modes_hbm.1) | copy-start | bytes 1572868
  1.7 0.9 %copy-start.1 = (bf16[256,512]{1,0:T(8,128)(2,1)S(1)}, bf16[256,512]{1,0:T(8,128)(2,1)}, u32[]{:S(2)}) copy-start(bf16[256,512]{1,0:T(8,128)(2,1)} %snaps_hbm.1) | copy-start | bytes 786436

commit v4 on v3

--- a/solution.py
+++ b/solution.py
@@ -40,19 +40,30 @@
         outer = [[lanes(rows[other], first + k) for k in range(8)] for other in range(group + 1, groups)]
         scaled = jnp.zeros((8, BLOCK), jnp.float32)
         diagonal = jnp.zeros((8, BLOCK), jnp.float32)
-        for j in range(8):
-            here = sub == j
-            column = columns[j]
-            root = lax.rsqrt(subs(column, j))
-            scaled_row = subs(panel, j) * root
-            scaled = jnp.where(here, scaled_row, scaled)
-            diagonal = jnp.where(here, root, diagonal)
-            pivot_row = jnp.where(lane == first + j, root, scaled_row) * root
-            weight = jnp.where(here, -1.0, column)
-            panel = jnp.where(here | (lane == first + j), 0.0, panel) - weight * pivot_row
-            for k in range(j + 1, 8):
-                entry = subs(columns[k], j) * (root * root)
-                columns[k] = jnp.where(here, 0.0, columns[k]) - weight * entry
+        for j in range(0, 8, 2):
+            at_left, at_right = lane == first + j, lane == first + j + 1
+            is_top, is_low = sub == j, sub == j + 1
+            pair = is_top | is_low
+            left, right = columns[j], columns[j + 1]
+            a, b, c = subs(left, j), subs(right, j), subs(right, j + 1)
+            root = lax.rsqrt(a * c - b * b)
+            inverse_det = root * root
+            root_a = lax.rsqrt(a)
+            top, low = subs(panel, j), subs(panel, j + 1)
+            low_factor = root_a * root
+            low_raw = jnp.where(at_left, -b, a * low - b * top)
+            scaled = jnp.where(is_top, top * root_a, jnp.where(is_low, low_raw * low_factor, scaled))
+            diagonal = jnp.where(is_top, root_a, jnp.where(is_low, a * low_factor, diagonal))
+            weight_top = jnp.where(pair, jnp.where(is_top, -1.0, 0.0), left)
+            weight_low = jnp.where(pair, jnp.where(is_low, -1.0, 0.0), right)
+            new_top = jnp.where(at_left, c, jnp.where(at_right, -b, c * top - b * low))
+            new_low = jnp.where(at_left, -b, jnp.where(at_right, a, a * low - b * top))
+            change = weight_top * new_top + weight_low * new_low
+            panel = jnp.where(pair | at_left | at_right, 0.0, panel) - change * inverse_det
+            for k in range(j + 2, 8):
+                top, low = subs(columns[k], j), subs(columns[k], j + 1)
+                change = weight_top * (c * top - b * low) + weight_low * (a * low - b * top)
+                columns[k] = jnp.where(pair, 0.0, columns[k]) - change * inverse_det
         row_index = sub + first
         upper.append(jnp.where(lane >= row_index, scaled, 0.0))
         inverse.append(jnp.where(lane < row_index, scaled, jnp.where(lane == row_index, diagonal, 0.0)))
@@ -299,7 +310,7 @@
             jax.ShapeDtypeStruct((rows, size), jnp.float32),
             jax.ShapeDtypeStruct((size, size), jnp.float32),
         ),
-        in_specs=[pl.BlockSpec(memory_space=pl.ANY)] * 2,
+        in_specs=[pl.BlockSpec(memory_space=pltpu.HBM)] * 2,
         out_specs=(pl.BlockSpec(memory_space=pltpu.VMEM),) * 2,
         scratch_shapes=[
             pltpu.VMEM((rows, modes), held_modes.dtype),
@@ -325,24 +336,32 @@
     size = gram_ref.shape[0]
     schur[...] = gram_ref[...]
     residual[...] = panel_ref[...]
-    column = lax.broadcasted_iota(jnp.int32, (BLOCK, size), 1)
-
-    def step(block, carry):
-        start = pl.multiple_of(block * BLOCK, BLOCK)
-        here = pl.ds(start, BLOCK)
-        rows = [schur[pl.ds(pl.multiple_of(start + 8 * g, 8), 8), here] for g in range(BLOCK // 8)]
-        upper, inverse = factor_block(rows)
-        beyond = dot(inverse, schur[here, :], (1, 0))
-        beyond = jnp.where(column >= start + BLOCK, beyond, 0.0)
-        schur[...] -= dot(beyond, beyond, (0, 0))
-        factor_ref[here, :] = beyond
-        factor_ref[here, here] = upper
+    index = lax.broadcasted_iota(jnp.int32, (BLOCK, BLOCK), 0)
+    on_diagonal = index == lax.broadcasted_iota(jnp.int32, (BLOCK, BLOCK), 1)
+    for start in range(0, size, BLOCK):
+        end = start + BLOCK
+        here = slice(start, end)
+        block = schur[here, here]
+        kept = jnp.where(on_diagonal, block, 0.0)
+        along = jnp.sum(kept, axis=0, keepdims=True)
+        scale = lax.rsqrt(along)
+        block = block * scale * lax.rsqrt(jnp.sum(kept, axis=1, keepdims=True))
+        upper, inverse = factor_block([block[8 * g : 8 * g + 8, :] for g in range(BLOCK // 8)])
+        inverse = inverse * scale
+        factor_ref[here, here] = upper * (along * scale)
+        if start:
+            factor_ref[here, :start] = jnp.zeros((BLOCK, start), jnp.float32)
+        if end < size:
+            beyond = dot(inverse, schur[here, end:], (1, 0))
+            factor_ref[here, end:] = beyond
+            for other in range(end, size, BLOCK):
+                rows = slice(other, other + BLOCK)
+                away = other - end
+                schur[rows, other:] -= dot(beyond[:, away : away + BLOCK], beyond[:, away:], (0, 0))
         part = dot(residual[:, here], inverse, (1, 1))
         basis_ref[:, here] = part
-        residual[...] -= dot(part, beyond, (1, 0))
-        return carry
-
-    lax.fori_loop(0, size // BLOCK, step, 0)
+        if end < size:
+            residual[:, end:] -= dot(part, beyond, (1, 0))
 
 
 def factor(gram, residual_panel):

time: 89.9 us -> 82.3 us (0.915)
  Pallas kernels: 87.1 us -> 79.5 us
    pallas_call x1, Pallas kernels: 27.3 us -> 19.6 us  [factor(): pl.pallas_call(factor_kernel, out_shape=(jax.ShapeDtypeStruct((rows, size...]
where the time goes in v4:
time: 82.3 us; the launch traced here: 82.1 us
  Pallas kernels  79.5 us (97%)
  local copies, waits for them, and re-layouts  1.98 us (2%)
    pallas_call x1, Pallas kernels, panel(): pl.pallas_call(functools.partial(panel_kernel, line_count, total_rows), o...  59.8 us
    pallas_call x1, Pallas kernels, factor(): pl.pallas_call(factor_kernel, out_shape=(jax.ShapeDtypeStruct((rows, size...  19.6 us
    unnamed x4, local copies, waits for them, and re-layouts  1.98 us

profile of v4, /device:TPU:1, one launch (start us, length us, event | category | flops | bytes accessed | tf_op | source)
XLA Modules:
  0.0 82.1 jit_solution(2568001981970333718)
XLA Ops:
  0.6 0.0 copy-start
  0.6 1.0 %copy-done = bf16[256,1024]{1,0:T(8,128)(2,1)S(1)} copy-done((bf16[256,1024]{1,0:T(8,128)(2,1)S(1)}, bf16[256,1024]{1,0:T(8,128)(2,1)}, u32[]{:S(2)}) %copy-start) | copy-done | bytes 524312
  1.7 0.0 copy-start.1
  1.7 0.9 %copy-done.1 = bf16[256,512]{1,0:T(8,128)(2,1)S(1)} copy-done((bf16[256,512]{1,0:T(8,128)(2,1)S(1)}, bf16[256,512]{1,0:T(8,128)(2,1)}, u32[]{:S(2)}) %copy-start.1) | copy-done | bytes 262168
  2.6 59.8 %panel.1 = (f32[256,512]{1,0:T(8,128)S(1)}, f32[512,512]{1,0:T(8,128)S(1)}) custom-call(bf16[256,1024]{1,0:T(8,128)(2,1)S(1)} %copy-done, bf16[256,512]{1,0:T(8,128)(2,1)S(1)} %copy-done.1), custom_call_target="tpu_custom_call" | custom-call | tf_op jit(solution)/shard_map/panel/pallas_call | solution.py:307
  62.5 19.6 %factor.1 = (f32[256,512]{1,0:T(8,128)}, f32[512,512]{1,0:T(8,128)}) custom-call(f32[512,512]{1,0:T(8,128)S(1)} %get-tuple-element.4.gram_ref, f32[256,512]{1,0:T(8,128)S(1)} %get-tuple-element.5.panel_ref), custom_call_target="tpu_custom_call" | custom-call | tf_op jit(solution)/shard_map/factor/pallas_call | solution.py:369
Async XLA Ops:
  0.6 1.0 %copy-start = (bf16[256,1024]{1,0:T(8,128)(2,1)S(1)}, bf16[256,1024]{1,0:T(8,128)(2,1)}, u32[]{:S(2)}) copy-start(bf16[256,1024]{1,0:T(8,128)(2,1)} %modes_hbm.1) | copy-start | bytes 1572868
  1.7 0.9 %copy-start.1 = (bf16[256,512]{1,0:T(8,128)(2,1)S(1)}, bf16[256,512]{1,0:T(8,128)(2,1)}, u32[]{:S(2)}) copy-start(bf16[256,512]{1,0:T(8,128)(2,1)} %snaps_hbm.1) | copy-start | bytes 786436

commit v5 on v4

--- a/solution.py
+++ b/solution.py
@@ -10,6 +10,7 @@
 BLOCK = 128
 MESH = pl.DeviceIdType.MESH
 CHUNKS = 2
+SPLIT = 2
 STEPS = 7
 HIGHEST = lax.Precision.HIGHEST
 
@@ -237,6 +238,7 @@
     entered = []
     size = residual_ref.shape[1]
     width = size // CHUNKS
+    narrow = width // SPLIT
 
     def coefficient_sum(chunk):
         acc = terms.at[chunk]
@@ -244,7 +246,7 @@
         def project(start, rows):
             wanted = modes_ref[:, pl.ds(pl.multiple_of(start, BLOCK), rows)]
             acc[slice_of(start, rows), :] = lax.dot_general(
-                wanted, snaps_ref[:, chunk * width : (chunk + 1) * width], (((0,), (0,)), ((), ())),
+                wanted, snaps_ref[:, chunk * narrow : (chunk + 1) * narrow], (((0,), (0,)), ((), ())),
                 preferred_element_type=jnp.float32,
             )
             if not entered:
@@ -260,7 +262,7 @@
         rows = pl.ds(0, (chunk + 1) * width)
         return all_reduce(
             gram_terms.at[chunk, rows], gram.at[chunk, rows], gram_landing.at[chunk], places, lambda start, n: None,
-            scale, send_sems.at[CHUNKS + chunk], recv_sems.at[CHUNKS + chunk], started,
+            scale, send_sems.at[SPLIT * CHUNKS + chunk], recv_sems.at[SPLIT * CHUNKS + chunk], started,
         )
 
     def times(part):
@@ -268,7 +270,7 @@
 
     def subtract(chunk):
         columns = slice(chunk * width, (chunk + 1) * width)
-        whole = coefficients[chunk]
+        whole = jnp.concatenate([coefficients[SPLIT * chunk + k] for k in range(SPLIT)], axis=1)
         high = whole.astype(jnp.bfloat16)
         rest = whole - high.astype(jnp.float32)
         middle = rest.astype(jnp.bfloat16)
@@ -278,13 +280,14 @@
         before = (chunk + 1) * width
         gram_terms[chunk, :before, :] = dot(residual_ref[:, :before], value, (0, 0))
 
-    sums = [coefficient_sum(chunk) for chunk in range(CHUNKS)]
+    sums = [coefficient_sum(chunk) for chunk in range(SPLIT * CHUNKS)]
     gram_sums = [gram_sum(chunk) for chunk in range(CHUNKS)]
     for _ in range(STEPS - 1):
         for turn in sums:
             next(turn)
     for chunk in range(CHUNKS):
-        next(sums[chunk], None)
+        for turn in sums[SPLIT * chunk : SPLIT * (chunk + 1)]:
+            next(turn, None)
         subtract(chunk)
         next(gram_sums[chunk])
     for _ in range(STEPS - 1):
@@ -316,14 +319,14 @@
             pltpu.VMEM((rows, modes), held_modes.dtype),
             pltpu.VMEM((rows, size), snapshots.dtype),
             pltpu.SemaphoreType.DMA((2,)),
-            pltpu.VMEM((CHUNKS, modes, width), jnp.float32),
-            pltpu.VMEM((CHUNKS, modes, width), jnp.float32),
-            pltpu.VMEM((CHUNKS, 2 * modes, width), jnp.float32),
+            pltpu.VMEM((SPLIT * CHUNKS, modes, width // SPLIT), jnp.float32),
+            pltpu.VMEM((SPLIT * CHUNKS, modes, width // SPLIT), jnp.float32),
+            pltpu.VMEM((SPLIT * CHUNKS, 2 * modes, width // SPLIT), jnp.float32),
             pltpu.VMEM((CHUNKS, size, width), jnp.float32),
             pltpu.VMEM((CHUNKS, size, width), jnp.float32),
             pltpu.VMEM((CHUNKS, 2 * size, width), jnp.float32),
-            pltpu.SemaphoreType.DMA((2 * CHUNKS, count)),
-            pltpu.SemaphoreType.DMA((2 * CHUNKS, count)),
+            pltpu.SemaphoreType.DMA(((SPLIT + 1) * CHUNKS, count)),
+            pltpu.SemaphoreType.DMA(((SPLIT + 1) * CHUNKS, count)),
         ],
         compiler_params=pltpu.CompilerParams(
             collective_id=0, has_side_effects=True, vmem_limit_bytes=40 * 1024 * 1024
@@ -387,7 +390,7 @@
     line_count = cells // 2
     unit = 8 * 4 * line_count
     halves = (held_modes.shape[1] // 2, size // CHUNKS // 2)
-    if slab == 4 and cells % 2 == 0 and size % (CHUNKS * BLOCK) == 0 and all(half % unit == 0 for half in halves):
+    if slab == 4 and cells % 2 == 0 and size % (SPLIT * CHUNKS * BLOCK) == 0 and all(half % unit == 0 for half in halves):
         return factor(*panel(held_modes, snapshots, line_count, total_rows)[::-1])
     local_terms = lax.dot_general(
         held_modes, snapshots, (((0,), (0,)), ((), ())), preferred_element_type=jnp.float32

time: 82.3 us -> 81.3 us (0.988)
  Pallas kernels: 79.5 us -> 78.5 us
    pallas_call x1, Pallas kernels: 59.8 us -> 58.8 us  [panel(): pl.pallas_call(functools.partial(panel_kernel, line_count, total_rows), o...]
where the time goes in v5:
time: 81.3 us; the launch traced here: 81.1 us
  Pallas kernels  78.5 us (97%)
  local copies, waits for them, and re-layouts  1.98 us (2%)
    pallas_call x1, Pallas kernels, panel(): pl.pallas_call(functools.partial(panel_kernel, line_count, total_rows), o...  58.8 us
    pallas_call x1, Pallas kernels, factor(): pl.pallas_call(factor_kernel, out_shape=(jax.ShapeDtypeStruct((rows, size...  19.6 us
    unnamed x4, local copies, waits for them, and re-layouts  1.98 us

profile of v5, /device:TPU:1, one launch (start us, length us, event | category | flops | bytes accessed | tf_op | source)
XLA Modules:
  0.0 81.1 jit_solution(2575521029578735339)
XLA Ops:
  0.6 0.0 copy-start
  0.6 1.0 %copy-done = bf16[256,1024]{1,0:T(8,128)(2,1)S(1)} copy-done((bf16[256,1024]{1,0:T(8,128)(2,1)S(1)}, bf16[256,1024]{1,0:T(8,128)(2,1)}, u32[]{:S(2)}) %copy-start) | copy-done | bytes 524312
  1.7 0.0 copy-start.1
  1.7 0.9 %copy-done.1 = bf16[256,512]{1,0:T(8,128)(2,1)S(1)} copy-done((bf16[256,512]{1,0:T(8,128)(2,1)S(1)}, bf16[256,512]{1,0:T(8,128)(2,1)}, u32[]{:S(2)}) %copy-start.1) | copy-done | bytes 262168
  2.6 58.8 %panel.1 = (f32[256,512]{1,0:T(8,128)S(1)}, f32[512,512]{1,0:T(8,128)S(1)}) custom-call(bf16[256,1024]{1,0:T(8,128)(2,1)S(1)} %copy-done, bf16[256,512]{1,0:T(8,128)(2,1)S(1)} %copy-done.1), custom_call_target="tpu_custom_call" | custom-call | tf_op jit(solution)/shard_map/panel/pallas_call | solution.py:310
  61.5 19.6 %factor.1 = (f32[256,512]{1,0:T(8,128)}, f32[512,512]{1,0:T(8,128)}) custom-call(f32[512,512]{1,0:T(8,128)S(1)} %get-tuple-element.4.gram_ref, f32[256,512]{1,0:T(8,128)S(1)} %get-tuple-element.5.panel_ref), custom_call_target="tpu_custom_call" | custom-call | tf_op jit(solution)/shard_map/factor/pallas_call | solution.py:372
Async XLA Ops:
  0.6 1.0 %copy-start = (bf16[256,1024]{1,0:T(8,128)(2,1)S(1)}, bf16[256,1024]{1,0:T(8,128)(2,1)}, u32[]{:S(2)}) copy-start(bf16[256,1024]{1,0:T(8,128)(2,1)} %modes_hbm.1) | copy-start | bytes 1572868
  1.7 0.9 %copy-start.1 = (bf16[256,512]{1,0:T(8,128)(2,1)S(1)}, bf16[256,512]{1,0:T(8,128)(2,1)}, u32[]{:S(2)}) copy-start(bf16[256,512]{1,0:T(8,128)(2,1)} %snaps_hbm.1) | copy-start | bytes 786436
